TPU v7x, 32 devices: a whole 2x2x4 slice. The times are simulated.
32 devices in a mesh: blk: 8 (over z, x), head: 4 (over y, core).
Axes of the slice: x: 2, y: 2, z: 4, core: 2. Of those that a mesh axis runs over, the one named last changes fastest.
Arguments:
- queries: bfloat16 [4096, 4096], P(('blk', 'head')), may hold values from -6 to 6
- keys: bfloat16 [4096, 512], P(('blk', 'head')), may hold values from -6 to 6
- values: bfloat16 [4096, 512], P(('blk', 'head')), may hold values from -12 to 12
- vertical: int32 [32, 8, 2], replicated, may hold values from -1 to 3, as said below
- near: int32 [32, 32], P(None, 'blk'), may hold values from -1 to 2, as said below
Outputs:
- attended: bfloat16 [4096, 4096], P(('blk', 'head'))
Inputs may be any that keep to these rules, and one draw needn't show every extreme that they name: vertical[h, r, c] is a key block of segment r counted from the segment's first block, or -1 for none; the two slots of one head and segment differ when neither is -1. near[h, n] is -1 or a block of the same segment as block n and strictly before it, counted from the segment's first block.
All inputs are finite; a program needn't handle non-finite values.
Results may differ from a plain program's by a relative error of at most 0.0055.
Values may be sent and summed in bfloat16 or wider, within the bound.
A program may use at most 64 MiB of HBM per device.

v0:
```python
import math

import jax
import jax.numpy as jnp
from jax import lax
from jax.sharding import PartitionSpec as P

QHEADS = 32
KVHEADS = 4
HEAD_DIM = 128
BLOCK = 128


def passed_along(block, axis, distance):
    devices = range(lax.axis_size(axis))
    route = [(i - distance, i) for i in devices if i - distance in devices]
    return lax.ppermute(block, axis, route)


def absorb(carried, scores, visible, value_tile, form):
    running, denominator, accumulated = carried
    masked = jnp.where(visible, scores, -jnp.inf)
    new_max = jnp.maximum(running, jnp.max(masked, axis=-1))
    shrink = jnp.exp(running - new_max)
    weights = jnp.where(visible, jnp.exp(masked - new_max[..., None]), 0.0)
    denominator = denominator * shrink + jnp.sum(weights, axis=-1)
    product = jnp.einsum(
        form, weights.astype(jnp.bfloat16), value_tile, preferred_element_type=jnp.float32
    )
    accumulated = accumulated * shrink[..., None] + product
    return (new_max, denominator, accumulated)


def far_state(query_rows, segment_of, far_keys, pair_live, blk_size, scaling):
    heads_here = query_rows.shape[0]
    row_count = query_rows.shape[1]
    group_cols = 4 * BLOCK
    source_ids = jnp.arange(2 * blk_size, dtype=jnp.int32) // 2
    pair_allowed = pair_live & (source_ids[None, :] < segment_of)
    column_allowed = jnp.repeat(pair_allowed, BLOCK, axis=1)
    initial = (
        jnp.full((heads_here, row_count), -1e30, jnp.float32),
        jnp.zeros((heads_here, row_count), jnp.float32),
        jnp.zeros((heads_here, row_count, HEAD_DIM), jnp.float32),
    )

    def group_step(group_index, state_now):
        first_col = group_index * group_cols
        key_tile = lax.dynamic_slice_in_dim(far_keys, first_col, group_cols, 1)
        allowed = lax.dynamic_slice_in_dim(column_allowed, first_col, group_cols, 1)
        scores = (
            jnp.einsum(
                "hqd,hkd->hqk",
                query_rows,
                key_tile[..., :HEAD_DIM],
                preferred_element_type=jnp.float32,
            )
            * scaling
        )
        return absorb(
            state_now, scores, allowed[:, None, :], key_tile[..., HEAD_DIM:], "hqk,hkd->hqd"
        )

    return lax.fori_loop(0, (segment_of + 1) // 2, group_step, initial)


def merge_states(first_state, second_state):
    top_value = jnp.maximum(first_state[0], second_state[0])
    keep_first = jnp.exp(first_state[0] - top_value)
    keep_second = jnp.exp(second_state[0] - top_value)
    denominator = first_state[1] * keep_first + second_state[1] * keep_second
    accumulated = first_state[2] * keep_first[..., None] + second_state[2] * keep_second[..., None]
    return (denominator, accumulated)


def local(queries, keys, values, vertical, near):
    heads_axis = lax.axis_size("head")
    blk_size = lax.axis_size("blk")
    tokens_dev = queries.shape[0]
    heads_here = QHEADS // heads_axis
    repeats = heads_axis // KVHEADS
    segment = tokens_dev * heads_axis
    blocks = segment // BLOCK
    scaling = 1.0 / math.sqrt(HEAD_DIM)
    head_index = lax.axis_index("head")
    blk_index = lax.axis_index("blk")
    ordering = jnp.arange(QHEADS, dtype=jnp.int32)
    local_q = queries.reshape(tokens_dev, QHEADS, HEAD_DIM)
    local_q = local_q.reshape(tokens_dev, heads_axis, heads_here * HEAD_DIM)
    local_k = jnp.repeat(keys.reshape(tokens_dev, KVHEADS, HEAD_DIM), repeats, axis=1)
    local_v = jnp.repeat(values.reshape(tokens_dev, KVHEADS, HEAD_DIM), repeats, axis=1)
    local_kv = jnp.concatenate([local_k, local_v], axis=2)
    segment_q, segment_kv = (
        lax.all_to_all(local_q, "head", split_axis=1, concat_axis=0, tiled=True),
        lax.all_to_all(local_kv, "head", split_axis=1, concat_axis=0, tiled=True),
    )
    segment_kv = segment_kv.reshape(segment, 2 * HEAD_DIM)
    mine = lax.dynamic_slice_in_dim(ordering, head_index * heads_here, heads_here)
    my_vertical = jnp.take(vertical, mine, axis=0)
    my_near = jnp.take(near, mine, axis=0)
    query_tiles = segment_q.reshape(blocks, BLOCK, heads_here, HEAD_DIM).transpose(2, 0, 1, 3)
    own_blocks = segment_kv.reshape(blocks, BLOCK, 2 * HEAD_DIM)
    within = jnp.arange(BLOCK, dtype=jnp.int32)
    causal = within[:, None] >= within[None, :]
    carried = (
        jnp.full((heads_here, blocks, BLOCK), -jnp.inf, jnp.float32),
        jnp.zeros((heads_here, blocks, BLOCK), jnp.float32),
        jnp.zeros((heads_here, blocks, BLOCK, HEAD_DIM), jnp.float32),
    )
    diag_scores = (
        jnp.einsum(
            "hnqd,nkd->hnqk",
            query_tiles,
            own_blocks[:, :, :HEAD_DIM],
            preferred_element_type=jnp.float32,
        )
        * scaling
    )
    carried = absorb(carried, diag_scores, causal, own_blocks[:, :, HEAD_DIM:], "hnqk,nkd->hnqd")
    near_tiles = own_blocks[jnp.maximum(my_near, 0)]
    near_scores = (
        jnp.einsum(
            "hnqd,hnkd->hnqk",
            query_tiles,
            near_tiles[..., :HEAD_DIM],
            preferred_element_type=jnp.float32,
        )
        * scaling
    )
    near_visible = (my_near >= 0)[:, :, None, None]
    carried = absorb(
        carried, near_scores, near_visible, near_tiles[..., HEAD_DIM:], "hnqk,hnkd->hnqd"
    )
    local_state = (
        carried[0].reshape(heads_here, segment),
        carried[1].reshape(heads_here, segment),
        carried[2].reshape(heads_here, segment, HEAD_DIM),
    )
    own_picked = lax.dynamic_index_in_dim(my_vertical, blk_index, 1, keepdims=False)
    own_tiles = own_blocks[jnp.maximum(own_picked, 0)]
    empty_buffer = jnp.zeros((heads_here, blk_size, 2, BLOCK, 2 * HEAD_DIM), jnp.bfloat16)
    buffer = lax.dynamic_update_index_in_dim(empty_buffer, own_tiles, blk_index, 1)

    def pass_turn(turn, loop_state):
        moving, held = loop_state
        moving = passed_along(moving, "blk", 1)
        source = (blk_index - turn) % blk_size
        picked = lax.dynamic_index_in_dim(my_vertical, source, 1, keepdims=False)
        pair_tiles = moving.reshape(blocks, BLOCK, 2 * HEAD_DIM)[jnp.maximum(picked, 0)]
        held = lax.dynamic_update_index_in_dim(held, pair_tiles, source, 1)
        return (moving, held)

    unused, buffer = lax.fori_loop(1, blk_size, pass_turn, (segment_kv, buffer))
    far_keys = buffer.reshape(heads_here, blk_size * 2 * BLOCK, 2 * HEAD_DIM)
    pair_live = (my_vertical >= 0).reshape(heads_here, 2 * blk_size)
    query_rows = query_tiles.reshape(heads_here, segment, HEAD_DIM)
    far_parts = far_state(query_rows, blk_index, far_keys, pair_live, blk_size, scaling)
    denominator, accumulated = merge_states(local_state, far_parts)
    finished = (accumulated / denominator[..., None]).astype(jnp.bfloat16)
    finished = finished.transpose(1, 0, 2).reshape(segment, 1, heads_here * HEAD_DIM)
    returned = lax.all_to_all(finished, "head", split_axis=0, concat_axis=1, tiled=True)
    returned = returned.reshape(tokens_dev, QHEADS, HEAD_DIM)
    return returned.reshape(tokens_dev, QHEADS * HEAD_DIM)


def solution(mesh):
    placed = (
        P(("blk", "head"), None),
        P(("blk", "head"), None),
        P(("blk", "head"), None),
        P(),
        P(None, "blk"),
    )
    return jax.shard_map(
        local, mesh=mesh, in_specs=placed, out_specs=P(("blk", "head"), None), check_vma=False
    )
```

profile of v0, /device:TPU:31, one launch (start us, length us, event | category | flops | bytes accessed | tf_op | source)
XLA Modules:
  0.0 203.2 jit_solution(17260133433883968460)
XLA Ops:
  3.2 4.2 %all-to-all-start = ((bf16[128,4,256]{2,0,1:T(8,128)(2,1)}), bf16[128,4,256]{2,0,1:T(8,128)(2,1)S(1)}, u32[]{:S(2)}, u32[]{:S(2)}) async-start(bf16[128,4,256]{2,0,1:T(8,128)(2,1)} %pad_maximum_fusion), calls=%async_computation | async-start | bytes 524288 | tf_op jit(solution)/shard_map/all_to_all | solution.py:95
  11.5 5.4 %all-to-all-start.1 = ((bf16[128,4,1024]{0,2,1:T(8,128)(2,1)}), bf16[128,4,1024]{0,2,1:T(8,128)(2,1)S(1)}, u32[]{:S(2)}, u32[]{:S(2)}) async-start(bf16[128,4,1024]{0,2,1:T(8,128)(2,1)} %bitcast.10), calls=%async_computation.1 | async-start | bytes 2097152 | tf_op jit(solution)/shard_map/all_to_all | solution.py:94
  18.7 3.2 %copy-done.1 = bf16[8,8,2,128,256]{4,3,2,0,1:T(8,128)(2,1)} copy-done((bf16[8,8,2,128,256]{4,3,2,0,1:T(8,128)(2,1)}, bf16[8,8,2,128,256]{4,3,2,0,1:T(8,128)(2,1)S(1)}, u32[]{:S(2)}) %copy-start.1) | copy-done | bytes 8388632
  21.9 70.3 %while.31 = (s32[]{:T(128)}, bf16[512,256]{1,0:T(8,128)(2,1)S(1)}, bf16[8,8,2,128,256]{4,3,2,0,1:T(8,128)(2,1)}, s32[]{:T(128)}, s32[8,8,2]{2,0,1:T(8,128)S(1)},...) while((s32[]{:T(128)}, bf16[512,256]{1,0:T(8,128)(2,1)S(1)}, bf16[8,8,2,128,256]{4,3,2,0,1:T(8,128)(2,1)}, ...), condition=%wide.region_3.4_spmd, body=%wide.region_2.3_spmd.sunk | while | flops 1057 | bytes 5771944 | solution.py:153
  23.3 8.0 %collective-permute-done = bf16[512,256]{1,0:T(8,128)(2,1)S(1)} collective-permute-done((bf16[512,256]{1,0:T(8,128)(2,1)S(1)}, bf16[512,256]{1,0:T(8,128)(2,1)S(1)}, u32[]{:S(2)}, u32[]{:S(2)}) %collective-permute-start) | collective-permute-done | bytes 262176 | tf_op jit(solution)/shard_map/while/body/eval_jaxpr/ppermute | solution.py:17
  34.5 7.1 %collective-permute-done = bf16[512,256]{1,0:T(8,128)(2,1)S(1)} collective-permute-done((bf16[512,256]{1,0:T(8,128)(2,1)S(1)}, bf16[512,256]{1,0:T(8,128)(2,1)S(1)}, u32[]{:S(2)}, u32[]{:S(2)}) %collective-permute-start) | collective-permute-done | bytes 262176 | tf_op jit(solution)/shard_map/while/body/eval_jaxpr/ppermute | solution.py:17
  44.7 7.1 %collective-permute-done = bf16[512,256]{1,0:T(8,128)(2,1)S(1)} collective-permute-done((bf16[512,256]{1,0:T(8,128)(2,1)S(1)}, bf16[512,256]{1,0:T(8,128)(2,1)S(1)}, u32[]{:S(2)}, u32[]{:S(2)}) %collective-permute-start) | collective-permute-done | bytes 262176 | tf_op jit(solution)/shard_map/while/body/eval_jaxpr/ppermute | solution.py:17
  54.9 6.3 %collective-permute-done = bf16[512,256]{1,0:T(8,128)(2,1)S(1)} collective-permute-done((bf16[512,256]{1,0:T(8,128)(2,1)S(1)}, bf16[512,256]{1,0:T(8,128)(2,1)S(1)}, u32[]{:S(2)}, u32[]{:S(2)}) %collective-permute-start) | collective-permute-done | bytes 262176 | tf_op jit(solution)/shard_map/while/body/eval_jaxpr/ppermute | solution.py:17
  64.3 6.6 %collective-permute-done = bf16[512,256]{1,0:T(8,128)(2,1)S(1)} collective-permute-done((bf16[512,256]{1,0:T(8,128)(2,1)S(1)}, bf16[512,256]{1,0:T(8,128)(2,1)S(1)}, u32[]{:S(2)}, u32[]{:S(2)}) %collective-permute-start) | collective-permute-done | bytes 262176 | tf_op jit(solution)/shard_map/while/body/eval_jaxpr/ppermute | solution.py:17
  74.0 6.6 %collective-permute-done = bf16[512,256]{1,0:T(8,128)(2,1)S(1)} collective-permute-done((bf16[512,256]{1,0:T(8,128)(2,1)S(1)}, bf16[512,256]{1,0:T(8,128)(2,1)S(1)}, u32[]{:S(2)}, u32[]{:S(2)}) %collective-permute-start) | collective-permute-done | bytes 262176 | tf_op jit(solution)/shard_map/while/body/eval_jaxpr/ppermute | solution.py:17
  83.7 6.7 %collective-permute-done = bf16[512,256]{1,0:T(8,128)(2,1)S(1)} collective-permute-done((bf16[512,256]{1,0:T(8,128)(2,1)S(1)}, bf16[512,256]{1,0:T(8,128)(2,1)S(1)}, u32[]{:S(2)}, u32[]{:S(2)}) %collective-permute-start) | collective-permute-done | bytes 262176 | tf_op jit(solution)/shard_map/while/body/eval_jaxpr/ppermute | solution.py:17
  92.2 7.7 %copy.96 = bf16[8,8,2,128,256]{4,3,2,1,0:T(8,128)(2,1)} copy(bf16[8,8,2,128,256]{4,3,2,0,1:T(8,128)(2,1)} %get-tuple-element.183) | data formatting | bytes 16777216 | tf_op jit(solution)/shard_map/while | solution.py:153
  104.7 57.0 %while.32 = (s32[]{:T(128)}, f32[8,512]{1,0:T(8,128)S(1)}, f32[8,512]{1,0:T(8,128)S(1)}, f32[8,512,128]{2,1,0:T(8,128)}, s32[]{:T(128)}, /*index=5*/pred[8,2048]...) while((s32[]{:T(128)}, f32[8,512]{1,0:T(8,128)S(1)}, ...), condition=%wide.region_7.8_spmd, body=%wide.region_4.7_spmd.sunk | while | flops 1102061568 | bytes 66347236 | solution.py:64
  104.7 3.3 %bitcast_reduce_fusion.3 = (f32[8,512]{1,0:T(8,128)S(1)}, f32[8,512,512]{2,1,0:T(8,128)S(1)}) fusion(pred[8,512]{1,0:T(8,128)(4,1)S(1)} %constant_dynamic-slice_fusion.2, bf16[8,512,128]{2,1,0:T(8,128)(2,1)S(1)} %get-tuple-element.397, bf16[8,2048,256]{2,1,0:T(8,128)(2,1)} %get-tuple-element.396, s32[]{:T(128)S(6)} %select_n.214), kind=kOutput, calls=%fused_computation.6.clone.1 | convolution fusion | flops 543158272 | bytes 10506244 | tf_op jit(solution)/shard_map/while/body/hqd,hkd->hqk/dot_general | solution.py:52
  108.1 2.4 %fusion.76 = f32[8,512]{1,0:T(8,128)S(1)} fusion(f32[8,512,512]{2,1,0:T(8,128)S(1)} %get-tuple-element.334, f32[8,512]{1,0:T(8,128)S(1)} %max.97, pred[8,512]{1,0:T(8,128)(4,1)S(1)} %constant_dynamic-slice_fusion.2), kind=kLoop, calls=%fused_computation.11.clone.1 | loop fusion | flops 10481664 | bytes 8425472 | tf_op jit(solution)/shard_map/while/body/reduce_sum | solution.py:26
  111.3 7.7 %multiply_add_fusion.5 = f32[8,512,128]{2,1,0:T(8,128)} fusion(f32[8,512,128]{2,1,0:T(8,128)} %get-tuple-element.380, f32[8,512,512]{2,1,0:T(8,128)} %copy-done, f32[8,512]{1,0:T(8,128)S(1)} %max.97, pred[8,512]{1,0:T(8,128)(4,1)S(1)} %constant_dynamic-slice_fusion.2, bf16[8,2048,256]{2,1,0:T(8,128)(2,1)} %get-tuple-element.396, s32[]{:T(128)S(6)} %select_n.214, ...), kind=kOutput, calls=%fused_computation.15.clone.1 | convolution fusion | flops 548405248 | bytes 13672456 | tf_op jit(solution)/shard_map/while/body/hqk,hkd->hqd/dot_general | solution.py:27
  118.9 3.3 %bitcast_reduce_fusion.3 = (f32[8,512]{1,0:T(8,128)S(1)}, f32[8,512,512]{2,1,0:T(8,128)S(1)}) fusion(pred[8,512]{1,0:T(8,128)(4,1)S(1)} %constant_dynamic-slice_fusion.2, bf16[8,512,128]{2,1,0:T(8,128)(2,1)S(1)} %get-tuple-element.397, bf16[8,2048,256]{2,1,0:T(8,128)(2,1)} %get-tuple-element.396, s32[]{:T(128)S(6)} %select_n.214), kind=kOutput, calls=%fused_computation.6.clone.1 | convolution fusion | flops 543158272 | bytes 10506244 | tf_op jit(solution)/shard_map/while/body/hqd,hkd->hqk/dot_general | solution.py:52
  125.5 7.7 %multiply_add_fusion.5 = f32[8,512,128]{2,1,0:T(8,128)} fusion(f32[8,512,128]{2,1,0:T(8,128)} %get-tuple-element.380, f32[8,512,512]{2,1,0:T(8,128)} %copy-done, f32[8,512]{1,0:T(8,128)S(1)} %max.97, pred[8,512]{1,0:T(8,128)(4,1)S(1)} %constant_dynamic-slice_fusion.2, bf16[8,2048,256]{2,1,0:T(8,128)(2,1)} %get-tuple-element.396, s32[]{:T(128)S(6)} %select_n.214, ...), kind=kOutput, calls=%fused_computation.15.clone.1 | convolution fusion | flops 548405248 | bytes 13672456 | tf_op jit(solution)/shard_map/while/body/hqk,hkd->hqd/dot_general | solution.py:27
  133.2 3.3 %bitcast_reduce_fusion.3 = (f32[8,512]{1,0:T(8,128)S(1)}, f32[8,512,512]{2,1,0:T(8,128)S(1)}) fusion(pred[8,512]{1,0:T(8,128)(4,1)S(1)} %constant_dynamic-slice_fusion.2, bf16[8,512,128]{2,1,0:T(8,128)(2,1)S(1)} %get-tuple-element.397, bf16[8,2048,256]{2,1,0:T(8,128)(2,1)} %get-tuple-element.396, s32[]{:T(128)S(6)} %select_n.214), kind=kOutput, calls=%fused_computation.6.clone.1 | convolution fusion | flops 543158272 | bytes 10506244 | tf_op jit(solution)/shard_map/while/body/hqd,hkd->hqk/dot_general | solution.py:52
  139.8 7.7 %multiply_add_fusion.5 = f32[8,512,128]{2,1,0:T(8,128)} fusion(f32[8,512,128]{2,1,0:T(8,128)} %get-tuple-element.380, f32[8,512,512]{2,1,0:T(8,128)} %copy-done, f32[8,512]{1,0:T(8,128)S(1)} %max.97, pred[8,512]{1,0:T(8,128)(4,1)S(1)} %constant_dynamic-slice_fusion.2, bf16[8,2048,256]{2,1,0:T(8,128)(2,1)} %get-tuple-element.396, s32[]{:T(128)S(6)} %select_n.214, ...), kind=kOutput, calls=%fused_computation.15.clone.1 | convolution fusion | flops 548405248 | bytes 13672456 | tf_op jit(solution)/shard_map/while/body/hqk,hkd->hqd/dot_general | solution.py:27
  147.4 3.3 %bitcast_reduce_fusion.3 = (f32[8,512]{1,0:T(8,128)S(1)}, f32[8,512,512]{2,1,0:T(8,128)S(1)}) fusion(pred[8,512]{1,0:T(8,128)(4,1)S(1)} %constant_dynamic-slice_fusion.2, bf16[8,512,128]{2,1,0:T(8,128)(2,1)S(1)} %get-tuple-element.397, bf16[8,2048,256]{2,1,0:T(8,128)(2,1)} %get-tuple-element.396, s32[]{:T(128)S(6)} %select_n.214), kind=kOutput, calls=%fused_computation.6.clone.1 | convolution fusion | flops 543158272 | bytes 10506244 | tf_op jit(solution)/shard_map/while/body/hqd,hkd->hqk/dot_general | solution.py:52
  154.0 7.7 %multiply_add_fusion.5 = f32[8,512,128]{2,1,0:T(8,128)} fusion(f32[8,512,128]{2,1,0:T(8,128)} %get-tuple-element.380, f32[8,512,512]{2,1,0:T(8,128)} %copy-done, f32[8,512]{1,0:T(8,128)S(1)} %max.97, pred[8,512]{1,0:T(8,128)(4,1)S(1)} %constant_dynamic-slice_fusion.2, bf16[8,2048,256]{2,1,0:T(8,128)(2,1)} %get-tuple-element.396, s32[]{:T(128)S(6)} %select_n.214, ...), kind=kOutput, calls=%fused_computation.15.clone.1 | convolution fusion | flops 548405248 | bytes 13672456 | tf_op jit(solution)/shard_map/while/body/hqk,hkd->hqd/dot_general | solution.py:27
  166.1 3.1 %fusion.24 = f32[8,4,128,128]{3,2,0,1:T(8,128)S(1)} fusion(f32[4,128,8,128]{1,3,2,0:T(8,128)S(1)} %fusion.31, f32[8,4,128,128]{3,2,0,1:T(8,128)S(1)} %get-tuple-element.245, bf16[8,4,128,128]{3,2,1,0:T(8,128)(2,1)S(1)} %copy-done.4, f32[8,4,128]{2,0,1:T(8,128)S(1)} %get-tuple-element.231, f32[8,4,128]{2,0,1:T(8,128)S(1)} %get-tuple-element.230, ...), kind=kOutput, calls=%fused_computation.40 | convolution fusion | flops 138412032 | bytes 7389216 | tf_op jit(solution)/shard_map/hnqk,hnkd->hnqd/dot_general | solution.py:27
  176.8 23.1 %all_to_all.45 = bf16[4,2,65536]{2,1,0:T(2,128)(2,1)S(1)} all-to-all(bf16[4,2,65536]{2,1,0:T(2,128)(2,1)S(1)} %reshape.223), channel_id=1, replica_groups=mesh['blk'=8,'head'=4] {'head'}, dimensions={0} | all-to-all | bytes 2097152 | tf_op jit(solution)/shard_map/all_to_all | solution.py:161
  (149 shorter events, 60.9 us)
Async XLA Ops:
  0.0 7.5 %copy-start.6 = (s32[32,8,2]{0,2,1:T(2,128)S(1)}, s32[32,8,2]{0,2,1:T(2,128)}, u32[]{:S(2)}) copy-start(s32[32,8,2]{0,2,1:T(2,128)} %param.12) | copy-start | bytes 6148
  0.0 8.3 %copy-start.7 = (s32[32,4]{0,1:T(4,128)S(1)}, s32[32,4]{0,1:T(4,128)}, u32[]{:S(2)}) copy-start(s32[32,4]{0,1:T(4,128)} %param.13) | copy-start | bytes 1540
  0.0 9.8 %copy-start.5 = (bf16[128,4096]{1,0:T(8,128)(2,1)S(1)}, bf16[128,4096]{1,0:T(8,128)(2,1)}, u32[]{:S(2)}) copy-start(bf16[128,4096]{1,0:T(8,128)(2,1)} %param.9) | copy-start | bytes 3145732
  3.2 8.3 %all-to-all-start = ((bf16[128,4,256]{2,0,1:T(8,128)(2,1)}), bf16[128,4,256]{2,0,1:T(8,128)(2,1)S(1)}, u32[]{:S(2)}, u32[]{:S(2)}) async-start(bf16[128,4,256]{2,0,1:T(8,128)(2,1)} %pad_maximum_fusion), calls=%async_computation | async-start | bytes 524288 | tf_op jit(solution)/shard_map/all_to_all | solution.py:95
  11.5 91.0 %all-to-all-start.1 = ((bf16[128,4,1024]{0,2,1:T(8,128)(2,1)}), bf16[128,4,1024]{0,2,1:T(8,128)(2,1)S(1)}, u32[]{:S(2)}, u32[]{:S(2)}) async-start(bf16[128,4,1024]{0,2,1:T(8,128)(2,1)} %bitcast.10), calls=%async_computation.1 | async-start | bytes 2097152 | tf_op jit(solution)/shard_map/all_to_all | solution.py:94
  18.7 3.2 %copy-start.1 = (bf16[8,8,2,128,256]{4,3,2,0,1:T(8,128)(2,1)}, bf16[8,8,2,128,256]{4,3,2,0,1:T(8,128)(2,1)S(1)}, u32[]{:S(2)}) copy-start(bf16[8,8,2,128,256]{4,3,2,0,1:T(8,128)(2,1)S(1)} %constant_dynamic-update-slice_fusion.1) | copy-start | bytes 25165828
  21.9 9.4 %collective-permute-start = (bf16[512,256]{1,0:T(8,128)(2,1)S(1)}, bf16[512,256]{1,0:T(8,128)(2,1)S(1)}, u32[]{:S(2)}, u32[]{:S(2)}) collective-permute-start(bf16[512,256]{1,0:T(8,128)(2,1)S(1)} %get-tuple-element.347), channel_id=1, source_target_pairs={{0,4},{4,8},{8,12},{12,16},{16,20},{20,24},{24,28},{1,5},{5,9},{9,... | collective-permute-start | bytes 786440 | tf_op jit(solution)/shard_map/while/body/eval_jaxpr/ppermute | solution.py:17
  33.0 8.5 %collective-permute-start = (bf16[512,256]{1,0:T(8,128)(2,1)S(1)}, bf16[512,256]{1,0:T(8,128)(2,1)S(1)}, u32[]{:S(2)}, u32[]{:S(2)}) collective-permute-start(bf16[512,256]{1,0:T(8,128)(2,1)S(1)} %get-tuple-element.347), channel_id=1, source_target_pairs={{0,4},{4,8},{8,12},{12,16},{16,20},{20,24},{24,28},{1,5},{5,9},{9,... | collective-permute-start | bytes 786440 | tf_op jit(solution)/shard_map/while/body/eval_jaxpr/ppermute | solution.py:17
  43.2 8.5 %collective-permute-start = (bf16[512,256]{1,0:T(8,128)(2,1)S(1)}, bf16[512,256]{1,0:T(8,128)(2,1)S(1)}, u32[]{:S(2)}, u32[]{:S(2)}) collective-permute-start(bf16[512,256]{1,0:T(8,128)(2,1)S(1)} %get-tuple-element.347), channel_id=1, source_target_pairs={{0,4},{4,8},{8,12},{12,16},{16,20},{20,24},{24,28},{1,5},{5,9},{9,... | collective-permute-start | bytes 786440 | tf_op jit(solution)/shard_map/while/body/eval_jaxpr/ppermute | solution.py:17
  53.5 7.7 %collective-permute-start = (bf16[512,256]{1,0:T(8,128)(2,1)S(1)}, bf16[512,256]{1,0:T(8,128)(2,1)S(1)}, u32[]{:S(2)}, u32[]{:S(2)}) collective-permute-start(bf16[512,256]{1,0:T(8,128)(2,1)S(1)} %get-tuple-element.347), channel_id=1, source_target_pairs={{0,4},{4,8},{8,12},{12,16},{16,20},{20,24},{24,28},{1,5},{5,9},{9,... | collective-permute-start | bytes 786440 | tf_op jit(solution)/shard_map/while/body/eval_jaxpr/ppermute | solution.py:17
  62.9 8.0 %collective-permute-start = (bf16[512,256]{1,0:T(8,128)(2,1)S(1)}, bf16[512,256]{1,0:T(8,128)(2,1)S(1)}, u32[]{:S(2)}, u32[]{:S(2)}) collective-permute-start(bf16[512,256]{1,0:T(8,128)(2,1)S(1)} %get-tuple-element.347), channel_id=1, source_target_pairs={{0,4},{4,8},{8,12},{12,16},{16,20},{20,24},{24,28},{1,5},{5,9},{9,... | collective-permute-start | bytes 786440 | tf_op jit(solution)/shard_map/while/body/eval_jaxpr/ppermute | solution.py:17
  72.6 8.0 %collective-permute-start = (bf16[512,256]{1,0:T(8,128)(2,1)S(1)}, bf16[512,256]{1,0:T(8,128)(2,1)S(1)}, u32[]{:S(2)}, u32[]{:S(2)}) collective-permute-start(bf16[512,256]{1,0:T(8,128)(2,1)S(1)} %get-tuple-element.347), channel_id=1, source_target_pairs={{0,4},{4,8},{8,12},{12,16},{16,20},{20,24},{24,28},{1,5},{5,9},{9,... | collective-permute-start | bytes 786440 | tf_op jit(solution)/shard_map/while/body/eval_jaxpr/ppermute | solution.py:17
  82.3 8.1 %collective-permute-start = (bf16[512,256]{1,0:T(8,128)(2,1)S(1)}, bf16[512,256]{1,0:T(8,128)(2,1)S(1)}, u32[]{:S(2)}, u32[]{:S(2)}) collective-permute-start(bf16[512,256]{1,0:T(8,128)(2,1)S(1)} %get-tuple-element.347), channel_id=1, source_target_pairs={{0,4},{4,8},{8,12},{12,16},{16,20},{20,24},{24,28},{1,5},{5,9},{9,... | collective-permute-start | bytes 786440 | tf_op jit(solution)/shard_map/while/body/eval_jaxpr/ppermute | solution.py:17
  108.0 3.2 %copy-start = (f32[8,512,512]{2,1,0:T(8,128)}, f32[8,512,512]{2,1,0:T(8,128)S(1)}, u32[]{:S(2)}) copy-start(f32[8,512,512]{2,1,0:T(8,128)S(1)} %get-tuple-element.334) | copy-start | bytes 25165828 | tf_op jit(solution)/shard_map/while
  122.3 3.2 %copy-start = (f32[8,512,512]{2,1,0:T(8,128)}, f32[8,512,512]{2,1,0:T(8,128)S(1)}, u32[]{:S(2)}) copy-start(f32[8,512,512]{2,1,0:T(8,128)S(1)} %get-tuple-element.334) | copy-start | bytes 25165828 | tf_op jit(solution)/shard_map/while
  136.5 3.2 %copy-start = (f32[8,512,512]{2,1,0:T(8,128)}, f32[8,512,512]{2,1,0:T(8,128)S(1)}, u32[]{:S(2)}) copy-start(f32[8,512,512]{2,1,0:T(8,128)S(1)} %get-tuple-element.334) | copy-start | bytes 25165828 | tf_op jit(solution)/shard_map/while
  150.8 3.2 %copy-start = (f32[8,512,512]{2,1,0:T(8,128)}, f32[8,512,512]{2,1,0:T(8,128)S(1)}, u32[]{:S(2)}) copy-start(f32[8,512,512]{2,1,0:T(8,128)S(1)} %get-tuple-element.334) | copy-start | bytes 25165828 | tf_op jit(solution)/shard_map/while
  161.7 1.2 copy-start.3
  164.5 1.6 copy-start.4
  169.3 1.6 copy-start.2
where the time goes:
time: 205 us; the launch traced here: 203 us
  matrix products  48.8 us (24%)
  waiting for transfers between devices  48.3 us (24%)
  local copies, waits for them, and re-layouts  47.1 us (23%)
  blocking collectives  23.1 us (11%)
  starting transfers between devices  18.6 us (9%)
  other arithmetic  16.5 us (8%)
    ppermute x7, waiting for transfers between devices, passed_along(): return lax.ppermute(block, axis, route)  48.2 us
    dot_general x6, matrix products, absorb(): jnp.einsum(form, weights.astype(jnp.bfloat16), value_tile, preferred_elem...  34.5 us
    all_to_all x1, blocking collectives, local(): lax.all_to_all(finished, 'head', split_axis=0, concat_axis=1, tiled=True)  23.1 us
    dot_general x4, matrix products, group_step(): jnp.einsum('hqd,hkd->hqk', query_rows, key_tile[..., :HEAD_DIM], preferre...  13.4 us
    unnamed x24, local copies, waits for them, and re-layouts  11.4 us
    reduce_sum x5, other arithmetic, absorb(): denominator = denominator * shrink + jnp.sum(weights, axis=-1)  11.3 us
    ppermute x7, starting transfers between devices, passed_along(): return lax.ppermute(block, axis, route)  9.03 us
    while x2, local copies, waits for them, and re-layouts, local(): unused, buffer = lax.fori_loop(1, blk_size, pass_turn, (segment_kv, buffer))  7.84 us
  transfers between devices with their start and end apart: 9, of which 8 were waited for; matrix products, arithmetic and copies ran while one was open for 14% of the time, Pallas kernels for 0%

commit v1 on v0

v1 whole, which is shorter than its diff:
```python
import functools
import math

import jax
import jax.numpy as jnp
from jax import lax
from jax.experimental import pallas as pl
from jax.experimental.pallas import tpu as pltpu
from jax.sharding import PartitionSpec as P

QHEADS = 32
KVHEADS = 4
HEAD_DIM = 128
BLOCK = 128
NEG = -1e30
EXP2_SCALE = math.log2(math.e) / math.sqrt(HEAD_DIM)
MESH = pl.DeviceIdType.MESH
CONTRACT_LAST = (((1,), (1,)), ((), ()))


def scores_of(query_rows, key_rows):
    return lax.dot_general(
        query_rows, key_rows, CONTRACT_LAST, preferred_element_type=jnp.float32
    )


def kernel(
    nb, nh, q_ref, k_ref, v_ref, vert_ref, near_ref, out_ref,
    qbuf, own, far, obuf,
    kv_send, kv_recv, q_send, q_recv, z_send, z_recv, x_send, x_recv, o_send, o_recv,
):
    b = lax.axis_index("blk")
    h = lax.axis_index("head")
    hh = QHEADS // nh
    rep = nh // KVHEADS
    half = nb // 2
    width = hh * HEAD_DIM
    odd = lax.rem(b, 2)
    partner = b + 1 - 2 * odd

    def lanes(index, size):
        return pl.ds(pl.multiple_of(index * size, size), size)

    def peer(d):
        return lax.rem(h + d, nh)

    barrier = pltpu.get_barrier_semaphore()
    for d in range(1, nh):
        pl.semaphore_signal(barrier, inc=1, device_id=(b, peer(d)), device_id_type=MESH)
    pl.semaphore_signal(barrier, inc=1, device_id=(partner, h), device_id_type=MESH)

    @pl.when(b + 2 < nb)
    def _():
        pl.semaphore_signal(barrier, inc=1, device_id=(b + 2, h), device_id_type=MESH)

    @pl.when(b >= 2)
    def _():
        pl.semaphore_signal(barrier, inc=1, device_id=(b - 2, h), device_id_type=MESH)

    mine = lax.div(h, rep)
    own[0, h] = k_ref[:, lanes(mine, HEAD_DIM)]
    own[1, h] = v_ref[:, lanes(mine, HEAD_DIM)]
    qbuf[h] = q_ref[:, lanes(h, width)]

    pl.semaphore_wait(
        barrier, nh + (b + 2 < nb).astype(jnp.int32) + (b >= 2).astype(jnp.int32)
    )

    def kv_copy(d, part):
        target = peer(d)
        source = (k_ref, v_ref)[part]
        return pltpu.make_async_remote_copy(
            src_ref=source.at[:, lanes(lax.div(target, rep), HEAD_DIM)],
            dst_ref=own.at[part, h],
            send_sem=kv_send.at[part, d - 1],
            recv_sem=kv_recv.at[part, d - 1],
            device_id=(b, target),
            device_id_type=MESH,
        )

    def q_copy(d):
        target = peer(d)
        return pltpu.make_async_remote_copy(
            src_ref=q_ref.at[:, lanes(target, width)],
            dst_ref=qbuf.at[h],
            send_sem=q_send.at[d - 1],
            recv_sem=q_recv.at[d - 1],
            device_id=(b, target),
            device_id_type=MESH,
        )

    def piece(j):
        return own if j == 0 else far.at[b - 2 * j]

    def z_copy(j):
        return pltpu.make_async_remote_copy(
            src_ref=piece(j),
            dst_ref=far.at[b - 2 * j],
            send_sem=z_send.at[j],
            recv_sem=z_recv.at[j],
            device_id=(b + 2, h),
            device_id_type=MESH,
        )

    def x_copy(j):
        return pltpu.make_async_remote_copy(
            src_ref=piece(j),
            dst_ref=far.at[b - 2 * j],
            send_sem=x_send.at[j],
            recv_sem=x_recv.at[j],
            device_id=(partner, h),
            device_id_type=MESH,
        )

    def arrival(slot, sem):
        return pltpu.make_async_remote_copy(
            src_ref=far.at[slot], dst_ref=far.at[slot], send_sem=sem, recv_sem=sem,
            device_id=(partner, h), device_id_type=MESH,
        )

    for part in range(2):
        for d in range(1, nh):
            kv_copy(d, part).start()
    for d in range(1, nh):
        q_copy(d).start()
    for part in range(2):
        for d in range(1, nh):
            kv_copy(d, part).wait_recv()

    def z_sends(j):
        return jnp.logical_and(b - 2 * j >= 0, b + 2 < nb)

    def x_sends(j):
        return b - 2 * j >= 0 if j else odd == 0

    for j in range(half):
        if j:
            @pl.when(b - 2 * j >= 0)
            def _():
                arrival(b - 2 * j, z_recv.at[j - 1]).wait_recv()

        @pl.when(z_sends(j))
        def _():
            z_copy(j).start()

        @pl.when(x_sends(j))
        def _():
            x_copy(j).start()

    for d in range(1, nh):
        q_copy(d).wait_recv()
    for j in range(half):
        @pl.when(partner - 2 * j >= 0 if j else odd == 1)
        def _():
            arrival(partner - 2 * j, x_recv.at[j]).wait_recv()

    tile_blocks = min(4, nh)
    rows = tile_blocks * BLOCK
    row_id = lax.broadcasted_iota(jnp.int32, (BLOCK, 2 * BLOCK), 0)
    col_id = lax.broadcasted_iota(jnp.int32, (BLOCK, 2 * BLOCK), 1)
    causal_bias = jnp.where(jnp.logical_and(col_id < BLOCK, row_id < col_id), NEG, 0.0)
    lane_id = lax.broadcasted_iota(jnp.int32, (1, 2 * BLOCK), 1)
    wide_id = lax.broadcasted_iota(jnp.int32, (1, 4 * BLOCK), 1)

    def o_copy(g, d):
        target = peer(d)
        return pltpu.make_async_remote_copy(
            src_ref=obuf.at[g, target],
            dst_ref=out_ref.at[:, lanes(h * hh + g, HEAD_DIM)],
            send_sem=o_send.at[g, d - 1],
            recv_sem=o_recv.at[g, d - 1],
            device_id=(b, target),
            device_id_type=MESH,
        )

    def head_step(g, carry):
        head = h * hh + g
        for tile in range(nh // tile_blocks):
            tops, sums, totals, queries = [], [], [], []
            for i in range(tile_blocks):
                n = tile * tile_blocks + i
                query = qbuf[n, :, lanes(g, HEAD_DIM)]
                queries.append(query)
                listed = near_ref[head, n]
                pick = jnp.maximum(listed, 0)
                key_rows = jnp.concatenate([own[0, n], own[0, pick]], axis=0)
                value_rows = jnp.concatenate([own[1, n], own[1, pick]], axis=0)
                gone = jnp.where(listed >= 0, 0.0, NEG)
                bias = causal_bias + jnp.where(lane_id < BLOCK, 0.0, gone)
                s = scores_of(query, key_rows) + bias
                top = jnp.max(s, axis=1, keepdims=True)
                w = jnp.exp2((s - top) * EXP2_SCALE)
                tops.append(top)
                sums.append(jnp.sum(w, axis=1, keepdims=True))
                totals.append(
                    jnp.dot(w.astype(jnp.bfloat16), value_rows, preferred_element_type=jnp.float32)
                )
            query_rows = jnp.concatenate(queries, axis=0)

            def far_step(t, state):
                top, total_w, acc = state
                keys_here, values_here = [], []
                bias = jnp.zeros((1, 4 * BLOCK), jnp.float32)
                for e in range(4):
                    r = 2 * t + e // 2
                    listed = vert_ref[head, r, e % 2]
                    pick = jnp.maximum(listed, 0)
                    slot = jnp.minimum(r, b - 1)
                    keys_here.append(far[slot, 0, pick])
                    values_here.append(far[slot, 1, pick])
                    live = jnp.logical_and(listed >= 0, r < b)
                    gone = jnp.where(live, 0.0, NEG)
                    inside = jnp.logical_and(wide_id >= e * BLOCK, wide_id < (e + 1) * BLOCK)
                    bias = jnp.where(inside, gone, bias)
                s = scores_of(query_rows, jnp.concatenate(keys_here, axis=0)) + bias
                new_top = jnp.maximum(top, jnp.max(s, axis=1, keepdims=True))
                shrink = jnp.exp2((top - new_top) * EXP2_SCALE)
                w = jnp.exp2((s - new_top) * EXP2_SCALE)
                total_w = total_w * shrink + jnp.sum(w, axis=1, keepdims=True)
                acc = acc * shrink + jnp.dot(
                    w.astype(jnp.bfloat16),
                    jnp.concatenate(values_here, axis=0),
                    preferred_element_type=jnp.float32,
                )
                return new_top, total_w, acc

            state = tuple(jnp.concatenate(x, axis=0) for x in (tops, sums, totals))
            _, total_w, acc = lax.fori_loop(0, lax.div(b + 1, 2), far_step, state)
            done = (acc / total_w).astype(jnp.bfloat16)
            for i in range(tile_blocks):
                obuf[g, tile * tile_blocks + i] = done[i * BLOCK : (i + 1) * BLOCK]
        out_ref[:, lanes(head, HEAD_DIM)] = obuf[g, h]
        for d in range(1, nh):
            o_copy(g, d).start()
        return carry

    lax.fori_loop(0, hh, head_step, 0)

    def finish(g, carry):
        for d in range(1, nh):
            pltpu.make_async_remote_copy(
                src_ref=obuf.at[g, h],
                dst_ref=out_ref.at[:, lanes(lax.rem(h + nh - d, nh) * hh + g, HEAD_DIM)],
                send_sem=o_send.at[g, d - 1],
                recv_sem=o_recv.at[g, d - 1],
                device_id=(b, peer(d)),
                device_id_type=MESH,
            ).wait_recv()
            o_copy(g, d).wait_send()
        return carry

    lax.fori_loop(0, hh, finish, 0)
    for d in range(1, nh):
        kv_copy(d, 0).wait_send()
        kv_copy(d, 1).wait_send()
        q_copy(d).wait_send()
    for j in range(half):
        @pl.when(z_sends(j))
        def _():
            z_copy(j).wait_send()

        @pl.when(x_sends(j))
        def _():
            x_copy(j).wait_send()


def local(queries, keys, values, vertical, near):
    nh = lax.axis_size("head")
    nb = lax.axis_size("blk")
    hh = QHEADS // nh
    assert queries.shape[0] == BLOCK and nb % 2 == 0 and nh % KVHEADS == 0
    half = nb // 2
    dma = pltpu.SemaphoreType.DMA
    vmem = pl.BlockSpec(memory_space=pltpu.VMEM)
    smem = pl.BlockSpec(memory_space=pltpu.SMEM)
    return pl.pallas_call(
        functools.partial(kernel, nb, nh),
        out_shape=jax.ShapeDtypeStruct((BLOCK, QHEADS * HEAD_DIM), jnp.bfloat16),
        in_specs=[vmem, vmem, vmem, smem, smem],
        out_specs=vmem,
        scratch_shapes=[
            pltpu.VMEM((nh, BLOCK, hh * HEAD_DIM), jnp.bfloat16),
            pltpu.VMEM((2, nh, BLOCK, HEAD_DIM), jnp.bfloat16),
            pltpu.VMEM((nb, 2, nh, BLOCK, HEAD_DIM), jnp.bfloat16),
            pltpu.VMEM((hh, nh, BLOCK, HEAD_DIM), jnp.bfloat16),
            dma((2, nh - 1)),
            dma((2, nh - 1)),
            dma((nh - 1,)),
            dma((nh - 1,)),
            dma((half,)),
            dma((half,)),
            dma((half,)),
            dma((half,)),
            dma((hh, nh - 1)),
            dma((hh, nh - 1)),
        ],
        compiler_params=pltpu.CompilerParams(
            collective_id=0, has_side_effects=True, vmem_limit_bytes=48 * 1024 * 1024
        ),
    )(queries, keys, values, vertical, near)


def solution(mesh):
    placed = (
        P(("blk", "head"), None),
        P(("blk", "head"), None),
        P(("blk", "head"), None),
        P(),
        P(None, "blk"),
    )
    return jax.shard_map(
        local, mesh=mesh, in_specs=placed, out_specs=P(("blk", "head"), None), check_vma=False
    )
```

time: 205 us -> 95.6 us (0.47)
  Pallas kernels: 0 us -> 91.4 us
  matrix products: 48.8 us -> 0 us
  waiting for transfers between devices: 48.3 us -> 0 us
  local copies, waits for them, and re-layouts: 47.1 us -> 4.04 us
  blocking collectives: 23.1 us -> 0 us
  starting transfers between devices: 18.6 us -> 0 us
  other arithmetic: 16.5 us -> 0 us
    pallas_call x0 -> x1, Pallas kernels: none -> 91.4 us  [local(): pl.pallas_call(functools.partial(kernel, nb, nh), out_shape=jax.ShapeDtyp...]
    dot_general x12 -> x0, matrix products: 48.8 us -> none  [the longest x6 34.5 us: absorb(): jnp.einsum(form, weights.astype(jnp.bfloat16), value_tile, preferred_elem...]
    ppermute x7 -> x0, waiting for transfers between devices: 48.2 us -> none  [passed_along(): return lax.ppermute(block, axis, route)]
    all_to_all x1 -> x0, blocking collectives: 23.1 us -> none  [local(): lax.all_to_all(finished, 'head', split_axis=0, concat_axis=1, tiled=True)]
    reduce_sum x5 -> x0, other arithmetic: 11.3 us -> none  [absorb(): denominator = denominator * shrink + jnp.sum(weights, axis=-1)]
    while x21 -> x0, local copies, waits for them, and re-layouts: 10.9 us -> none  [the longest x2 7.84 us: local(): unused, buffer = lax.fori_loop(1, blk_size, pass_turn, (segment_kv, buffer))]
    all_to_all x2 -> x0, starting transfers between devices: 9.59 us -> none  [the longest x1 5.4 us: local(): lax.all_to_all(local_q, 'head', split_axis=1, concat_axis=0, tiled=True)]
    ppermute x7 -> x0, starting transfers between devices: 9.03 us -> none  [passed_along(): return lax.ppermute(block, axis, route)]
  transfers between devices with their start and end apart: 9 -> 0, of which waited for: 8 -> 0; matrix products, arithmetic and copies ran while one was open for 14% -> 0% of each run, Pallas kernels for 0% -> 0%
where the time goes in v1:
time: 95.6 us; the launch traced here: 95.4 us
  Pallas kernels  91.4 us (96%)
  local copies, waits for them, and re-layouts  4.04 us (4%)
    pallas_call x1, Pallas kernels, local(): pl.pallas_call(functools.partial(kernel, nb, nh), out_shape=jax.ShapeDtyp...  91.4 us
    unnamed x11, local copies, waits for them, and re-layouts  4.04 us

profile of v1, /device:TPU:31, one launch (start us, length us, event | category | flops | bytes accessed | tf_op | source)
XLA Modules:
  0.0 95.4 jit_solution(17387968965091205762)
XLA Ops:
  0.0 0.0 copy-start.3
  0.0 0.0 copy-start.1
  0.0 0.8 copy.7.near_ref
  0.8 0.0 copy-done.3
  0.8 0.1 copy.6.vert_ref
  0.9 0.0 copy-done.1
  1.0 0.0 copy-start
  1.0 1.2 %copy-done = bf16[128,4096]{1,0:T(8,128)(2,1)S(1)} copy-done((bf16[128,4096]{1,0:T(8,128)(2,1)S(1)}, bf16[128,4096]{1,0:T(8,128)(2,1)}, u32[]{:S(2)}) %copy-start) | copy-done | bytes 1048600
  2.2 0.0 copy-start.2
  2.2 0.9 copy-done.2
  3.1 91.4 %shard_map.55 = bf16[128,4096]{1,0:T(8,128)(2,1)S(1)} custom-call(bf16[128,4096]{1,0:T(8,128)(2,1)S(1)} %copy-done, bf16[128,512]{1,0:T(8,128)(2,1)S(1)} %copy-done.1, bf16[128,512]{1,0:T(8,128)(2,1)S(1)} %copy-done.2, s32[32,8,2]{2,1,0:T(8,128)S(1)} %copy.6.vert_ref, s32[32,4]{1,0:T(8,128)S(1)} %copy.7.near_ref), custom_call_target="tpu_custom_call" | custom-call | tf_op jit(solution)/shard_map/pallas_call | solution.py:276
  94.5 1.0 %copy.9 = bf16[128,4096]{1,0:T(8,128)(2,1)} copy(bf16[128,4096]{1,0:T(8,128)(2,1)S(1)} %shard_map.55) | data formatting | bytes 2097152
Async XLA Ops:
  0.0 0.8 copy-start.3
  0.0 0.9 copy-start.1
  1.0 1.2 %copy-start = (bf16[128,4096]{1,0:T(8,128)(2,1)S(1)}, bf16[128,4096]{1,0:T(8,128)(2,1)}, u32[]{:S(2)}) copy-start(bf16[128,4096]{1,0:T(8,128)(2,1)} %q_ref.1) | copy-start | bytes 3145732
  2.2 0.9 copy-start.2

commit v2 on v1

v2 whole, which is shorter than its diff:
```python
import functools
import math

import jax
import jax.numpy as jnp
from jax import lax
from jax.experimental import pallas as pl
from jax.experimental.pallas import tpu as pltpu
from jax.sharding import PartitionSpec as P

QHEADS = 32
KVHEADS = 4
HEAD_DIM = 128
BLOCK = 128
NEG = -1e30
EXP2_SCALE = math.log2(math.e) / math.sqrt(HEAD_DIM)
MESH = pl.DeviceIdType.MESH
CONTRACT_LAST = (((1,), (1,)), ((), ()))


def scores_of(query_rows, key_rows):
    return lax.dot_general(
        query_rows, key_rows, CONTRACT_LAST, preferred_element_type=jnp.float32
    )


def kernel(nb, nh, q_ref, k_ref, v_ref, vert_ref, near_ref, out_ref, *scratch):
    half = nb // 2
    far, scratch = scratch[:half], scratch[half:]
    qbuf, own, vturn, obuf, tops, sums, accs = scratch[:7]
    kv_send, kv_recv, q_send, q_recv, z_send, z_recv, x_send, x_recv, o_send, o_recv = scratch[7:]
    b = lax.axis_index("blk")
    h = lax.axis_index("head")
    hh = QHEADS // nh
    rep = nh // KVHEADS
    width = hh * HEAD_DIM
    odd = lax.rem(b, 2)
    partner = b + 1 - 2 * odd

    def lanes(index, size):
        return pl.ds(pl.multiple_of(index * size, size), size)

    def peer(d):
        return lax.rem(h + d, nh)

    barrier = pltpu.get_barrier_semaphore()
    for d in range(1, nh):
        pl.semaphore_signal(barrier, inc=1, device_id=(b, peer(d)), device_id_type=MESH)
    pl.semaphore_signal(barrier, inc=1, device_id=(partner, h), device_id_type=MESH)

    @pl.when(b + 2 < nb)
    def _():
        pl.semaphore_signal(barrier, inc=1, device_id=(b + 2, h), device_id_type=MESH)

    @pl.when(b >= 2)
    def _():
        pl.semaphore_signal(barrier, inc=1, device_id=(b - 2, h), device_id_type=MESH)

    mine = lax.div(h, rep)
    own[0, h] = k_ref[:, lanes(mine, HEAD_DIM)]
    for kv in range(KVHEADS):
        vturn[kv] = v_ref[:, kv * HEAD_DIM : (kv + 1) * HEAD_DIM].T
    own[1, h] = vturn[mine]
    qbuf[h] = q_ref[:, lanes(h, width)]

    pl.semaphore_wait(
        barrier, nh + (b + 2 < nb).astype(jnp.int32) + (b >= 2).astype(jnp.int32)
    )

    def kv_copy(d, part):
        target = peer(d)
        kv = lax.div(target, rep)
        return pltpu.make_async_remote_copy(
            src_ref=vturn.at[kv] if part else k_ref.at[:, lanes(kv, HEAD_DIM)],
            dst_ref=own.at[part, h],
            send_sem=kv_send.at[part, d - 1],
            recv_sem=kv_recv.at[part, d - 1],
            device_id=(b, target),
            device_id_type=MESH,
        )

    def q_copy(d):
        target = peer(d)
        return pltpu.make_async_remote_copy(
            src_ref=q_ref.at[:, lanes(target, width)],
            dst_ref=qbuf.at[h],
            send_sem=q_send.at[d - 1],
            recv_sem=q_recv.at[d - 1],
            device_id=(b, target),
            device_id_type=MESH,
        )

    def piece(j):
        return own if j == 0 else far[j - 1].at[1]

    def z_copy(j):
        return pltpu.make_async_remote_copy(
            src_ref=piece(j),
            dst_ref=far[j].at[1],
            send_sem=z_send.at[j],
            recv_sem=z_recv.at[j],
            device_id=(b + 2, h),
            device_id_type=MESH,
        )

    def x_copy(j, t):
        return pltpu.make_async_remote_copy(
            src_ref=piece(j),
            dst_ref=far[t].at[0],
            send_sem=x_send.at[j],
            recv_sem=x_recv.at[t],
            device_id=(partner, h),
            device_id_type=MESH,
        )

    def z_sends(j):
        return jnp.logical_and(b - 2 * j >= 0, b + 2 < nb)

    def pass_on(j):
        if j >= half:
            return
        if j:
            @pl.when(b - 2 * j >= 0)
            def _():
                z_copy(j - 1).wait_recv()

        @pl.when(z_sends(j))
        def _():
            z_copy(j).start()

        @pl.when(jnp.logical_and(odd == 0, b - 2 * j >= 0))
        def _():
            x_copy(j, j).start()

        if j:
            @pl.when(jnp.logical_and(odd == 1, b - 2 * j >= 0))
            def _():
                x_copy(j, j - 1).start()

    for part in range(2):
        for d in range(1, nh):
            kv_copy(d, part).start()
    for d in range(1, nh):
        q_copy(d).start()
    for part in range(2):
        for d in range(1, nh):
            kv_copy(d, part).wait_recv()

    pass_on(0)
    pass_on(1)
    for d in range(1, nh):
        q_copy(d).wait_recv()

    tile_blocks = min(4, nh)
    tiles = nh // tile_blocks
    key_id = lax.broadcasted_iota(jnp.int32, (BLOCK, BLOCK), 0)
    row_id = lax.broadcasted_iota(jnp.int32, (BLOCK, BLOCK), 1)
    causal_bias = jnp.where(key_id > row_id, NEG, 0.0)

    def o_copy(g, d):
        target = peer(d)
        return pltpu.make_async_remote_copy(
            src_ref=obuf.at[g, target],
            dst_ref=out_ref.at[:, lanes(h * hh + g, HEAD_DIM)],
            send_sem=o_send.at[g, d - 1],
            recv_sem=o_recv.at[g, d - 1],
            device_id=(b, target),
            device_id_type=MESH,
        )

    def weigh(s, shift):
        return jnp.exp2((s - shift) * EXP2_SCALE)

    def column_max(s):
        return jnp.max(s, axis=0, keepdims=True)

    def column_sum(w):
        return jnp.sum(w, axis=0, keepdims=True)

    def mix(values_turned, weights):
        joined = jnp.concatenate([w.astype(jnp.bfloat16) for w in weights], axis=0)
        return jnp.dot(
            jnp.concatenate(values_turned, axis=1), joined, preferred_element_type=jnp.float32
        )

    def near_step(g, carry):
        head = h * hh + g
        for n in range(nh):
            tile, at = n // tile_blocks, n % tile_blocks * BLOCK
            query = qbuf[n, :, lanes(g, HEAD_DIM)]
            listed = near_ref[head, n]
            live = listed >= 0
            pick = jnp.maximum(listed, 0)
            s0 = scores_of(own[0, n], query) + causal_bias
            s1 = scores_of(own[0, pick], query)
            top = jnp.maximum(column_max(s0), jnp.where(live, column_max(s1), NEG))
            w0 = weigh(s0, top)
            w1 = weigh(s1, jnp.where(live, top, -NEG))
            tops[g, tile, :, at : at + BLOCK] = top
            sums[g, tile, :, at : at + BLOCK] = column_sum(w0) + column_sum(w1)
            accs[g, tile, :, at : at + BLOCK] = mix([own[1, n], own[1, pick]], [w0, w1])
        return carry

    lax.fori_loop(0, hh, near_step, 0)

    for t in range(half):
        pass_on(t + 2)

        @pl.when(b - 1 - 2 * t >= 0)
        def _(t=t):
            x_copy(t, t).wait_recv()
            slots = (0, (b - 2 - 2 * t >= 0).astype(jnp.int32))

            def far_step(i, carry):
                g, tile = lax.div(i, tiles), lax.rem(i, tiles)
                head = h * hh + g
                query_rows = jnp.concatenate(
                    [
                        qbuf[tile * tile_blocks + n, :, lanes(g, HEAD_DIM)]
                        for n in range(tile_blocks)
                    ],
                    axis=0,
                )
                lives, values_turned, scores = [], [], []
                top = tops[g, tile]
                new_top = top
                for e in range(4):
                    r = b - 1 - 2 * t - e // 2
                    listed = vert_ref[head, jnp.maximum(r, 0), e % 2]
                    pick = jnp.maximum(listed, 0)
                    slot = slots[e // 2]
                    live = jnp.logical_and(listed >= 0, r >= 0)
                    lives.append(live)
                    values_turned.append(far[t][slot, 1, pick])
                    s = scores_of(far[t][slot, 0, pick], query_rows)
                    scores.append(s)
                    new_top = jnp.maximum(new_top, jnp.where(live, column_max(s), NEG))
                shrink = weigh(top, new_top)
                total = sums[g, tile] * shrink
                weights = []
                for live, s in zip(lives, scores):
                    w = weigh(s, jnp.where(live, new_top, -NEG))
                    total = total + column_sum(w)
                    weights.append(w)
                tops[g, tile] = new_top
                sums[g, tile] = total
                accs[g, tile] = accs[g, tile] * shrink + mix(values_turned, weights)
                return carry

            lax.fori_loop(0, hh * tiles, far_step, 0)

    def last_step(g, carry):
        for tile in range(tiles):
            done = (accs[g, tile] / sums[g, tile]).astype(jnp.bfloat16)
            for n in range(tile_blocks):
                obuf[g, tile * tile_blocks + n] = done[:, n * BLOCK : (n + 1) * BLOCK].T
        out_ref[:, lanes(h * hh + g, HEAD_DIM)] = obuf[g, h]
        for d in range(1, nh):
            o_copy(g, d).start()
        return carry

    lax.fori_loop(0, hh, last_step, 0)

    def finish(g, carry):
        for d in range(1, nh):
            pltpu.make_async_remote_copy(
                src_ref=obuf.at[g, h],
                dst_ref=out_ref.at[:, lanes(lax.rem(h + nh - d, nh) * hh + g, HEAD_DIM)],
                send_sem=o_send.at[g, d - 1],
                recv_sem=o_recv.at[g, d - 1],
                device_id=(b, peer(d)),
                device_id_type=MESH,
            ).wait_recv()
            o_copy(g, d).wait_send()
        return carry

    lax.fori_loop(0, hh, finish, 0)
    for d in range(1, nh):
        kv_copy(d, 0).wait_send()
        kv_copy(d, 1).wait_send()
        q_copy(d).wait_send()
    for j in range(half):
        @pl.when(z_sends(j))
        def _():
            z_copy(j).wait_send()

        @pl.when(b - 2 * j >= (0 if j else 2 * odd * nb))
        def _():
            x_copy(j, 0).wait_send()


def local(queries, keys, values, vertical, near):
    nh = lax.axis_size("head")
    nb = lax.axis_size("blk")
    hh = QHEADS // nh
    assert queries.shape[0] == BLOCK and nb % 2 == 0 and nh % KVHEADS == 0
    half = nb // 2
    tiles = nh // min(4, nh)
    dma = pltpu.SemaphoreType.DMA
    vmem = pl.BlockSpec(memory_space=pltpu.VMEM)
    smem = pl.BlockSpec(memory_space=pltpu.SMEM)
    return pl.pallas_call(
        functools.partial(kernel, nb, nh),
        out_shape=jax.ShapeDtypeStruct((BLOCK, QHEADS * HEAD_DIM), jnp.bfloat16),
        in_specs=[vmem, vmem, vmem, smem, smem],
        out_specs=vmem,
        scratch_shapes=[pltpu.VMEM((2, 2, nh, BLOCK, HEAD_DIM), jnp.bfloat16)] * half
        + [
            pltpu.VMEM((nh, BLOCK, hh * HEAD_DIM), jnp.bfloat16),
            pltpu.VMEM((2, nh, BLOCK, HEAD_DIM), jnp.bfloat16),
            pltpu.VMEM((KVHEADS, HEAD_DIM, BLOCK), jnp.bfloat16),
            pltpu.VMEM((hh, nh, BLOCK, HEAD_DIM), jnp.bfloat16),
            pltpu.VMEM((hh, tiles, 1, nh // tiles * BLOCK), jnp.float32),
            pltpu.VMEM((hh, tiles, 1, nh // tiles * BLOCK), jnp.float32),
            pltpu.VMEM((hh, tiles, HEAD_DIM, nh // tiles * BLOCK), jnp.float32),
            dma((2, nh - 1)),
            dma((2, nh - 1)),
            dma((nh - 1,)),
            dma((nh - 1,)),
            dma((half,)),
            dma((half,)),
            dma((half,)),
            dma((half,)),
            dma((hh, nh - 1)),
            dma((hh, nh - 1)),
        ],
        compiler_params=pltpu.CompilerParams(
            collective_id=0, has_side_effects=True, vmem_limit_bytes=48 * 1024 * 1024
        ),
    )(queries, keys, values, vertical, near)


def solution(mesh):
    placed = (
        P(("blk", "head"), None),
        P(("blk", "head"), None),
        P(("blk", "head"), None),
        P(),
        P(None, "blk"),
    )
    return jax.shard_map(
        local, mesh=mesh, in_specs=placed, out_specs=P(("blk", "head"), None), check_vma=False
    )
```

time: 95.6 us -> 64.9 us (0.68)
  Pallas kernels: 91.4 us -> 60.7 us
    pallas_call x1, Pallas kernels: 91.4 us -> 60.7 us  [local(): pl.pallas_call(functools.partial(kernel, nb, nh), out_shape=jax.ShapeDtyp...]
where the time goes in v2:
time: 64.9 us; the launch traced here: 64.7 us
  Pallas kernels  60.7 us (94%)
  local copies, waits for them, and re-layouts  4.04 us (6%)
    pallas_call x1, Pallas kernels, local(): pl.pallas_call(functools.partial(kernel, nb, nh), out_shape=jax.ShapeDtyp...  60.7 us
    unnamed x11, local copies, waits for them, and re-layouts  4.04 us

profile of v2, /device:TPU:31, one launch (start us, length us, event | category | flops | bytes accessed | tf_op | source)
XLA Modules:
  0.0 64.7 jit_solution(5680124180204057140)
XLA Ops:
  0.0 0.0 copy-start.3
  0.0 0.0 copy-start.1
  0.0 0.8 %copy.7.near_ref = s32[32,4]{1,0:T(8,128)S(1)} copy(s32[32,4]{0,1:T(4,128)} %param.9) | data formatting | bytes 1024 | tf_op args[4]
  0.8 0.0 copy-done.3
  0.8 0.1 copy.6.vert_ref
  0.9 0.0 copy-done.1
  1.0 0.0 copy-start
  1.0 1.2 %copy-done = bf16[128,4096]{1,0:T(8,128)(2,1)S(1)} copy-done((bf16[128,4096]{1,0:T(8,128)(2,1)S(1)}, bf16[128,4096]{1,0:T(8,128)(2,1)}, u32[]{:S(2)}) %copy-start) | copy-done | bytes 1048600
  2.2 0.0 copy-start.2
  2.2 0.9 %copy-done.2 = bf16[128,512]{1,0:T(8,128)(2,1)S(1)} copy-done((bf16[128,512]{1,0:T(8,128)(2,1)S(1)}, bf16[128,512]{1,0:T(8,128)(2,1)}, u32[]{:S(2)}) %copy-start.2) | copy-done | bytes 131096
  3.1 60.7 %shard_map.55 = bf16[128,4096]{1,0:T(8,128)(2,1)S(1)} custom-call(bf16[128,4096]{1,0:T(8,128)(2,1)S(1)} %copy-done, bf16[128,512]{1,0:T(8,128)(2,1)S(1)} %copy-done.1, bf16[128,512]{1,0:T(8,128)(2,1)S(1)} %copy-done.2, s32[32,8,2]{2,1,0:T(8,128)S(1)} %copy.6.vert_ref, s32[32,4]{1,0:T(8,128)S(1)} %copy.7.near_ref), custom_call_target="tpu_custom_call" | custom-call | tf_op jit(solution)/shard_map/pallas_call | solution.py:302
  63.8 1.0 %copy.9 = bf16[128,4096]{1,0:T(8,128)(2,1)} copy(bf16[128,4096]{1,0:T(8,128)(2,1)S(1)} %shard_map.55) | data formatting | bytes 2097152
Async XLA Ops:
  0.0 0.8 %copy-start.3 = (s32[32,8,2]{0,2,1:T(2,128)S(1)}, s32[32,8,2]{0,2,1:T(2,128)}, u32[]{:S(2)}) copy-start(s32[32,8,2]{0,2,1:T(2,128)} %param.8) | copy-start | bytes 6148
  0.0 0.9 %copy-start.1 = (bf16[128,512]{1,0:T(8,128)(2,1)S(1)}, bf16[128,512]{1,0:T(8,128)(2,1)}, u32[]{:S(2)}) copy-start(bf16[128,512]{1,0:T(8,128)(2,1)} %k_ref.1) | copy-start | bytes 393220
  1.0 1.2 %copy-start = (bf16[128,4096]{1,0:T(8,128)(2,1)S(1)}, bf16[128,4096]{1,0:T(8,128)(2,1)}, u32[]{:S(2)}) copy-start(bf16[128,4096]{1,0:T(8,128)(2,1)} %q_ref.1) | copy-start | bytes 3145732
  2.2 0.9 %copy-start.2 = (bf16[128,512]{1,0:T(8,128)(2,1)S(1)}, bf16[128,512]{1,0:T(8,128)(2,1)}, u32[]{:S(2)}) copy-start(bf16[128,512]{1,0:T(8,128)(2,1)} %v_ref.1) | copy-start | bytes 393220

commit v3 on v2

--- a/solution.py
+++ b/solution.py
@@ -28,7 +28,8 @@
     half = nb // 2
     far, scratch = scratch[:half], scratch[half:]
     qbuf, own, vturn, obuf, tops, sums, accs = scratch[:7]
-    kv_send, kv_recv, q_send, q_recv, z_send, z_recv, x_send, x_recv, o_send, o_recv = scratch[7:]
+    kv_send, kv_recv, q_send, q_recv, z_send, z_recv, x_send, x_recv, o_send, o_recv = scratch[7:17]
+    local_sem = scratch[17]
     b = lax.axis_index("blk")
     h = lax.axis_index("head")
     hh = QHEADS // nh
@@ -61,7 +62,8 @@
     for kv in range(KVHEADS):
         vturn[kv] = v_ref[:, kv * HEAD_DIM : (kv + 1) * HEAD_DIM].T
     own[1, h] = vturn[mine]
-    qbuf[h] = q_ref[:, lanes(h, width)]
+    own_q = pltpu.make_async_copy(q_ref.at[:, lanes(h, width)], qbuf.at[h], local_sem)
+    own_q.start()
 
     pl.semaphore_wait(
         barrier, nh + (b + 2 < nb).astype(jnp.int32) + (b >= 2).astype(jnp.int32)
@@ -79,36 +81,37 @@
             device_id_type=MESH,
         )
 
-    def q_copy(d):
+    def q_copy(d, c):
         target = peer(d)
-        return pltpu.make_async_remote_copy(
-            src_ref=q_ref.at[:, lanes(target, width)],
-            dst_ref=qbuf.at[h],
-            send_sem=q_send.at[d - 1],
-            recv_sem=q_recv.at[d - 1],
+        part = width // 2
+        return pltpu.make_async_remote_copy(
+            src_ref=q_ref.at[:, pl.ds(pl.multiple_of(target * width + c * part, part), part)],
+            dst_ref=qbuf.at[h, :, pl.ds(c * part, part)],
+            send_sem=q_send.at[c, d - 1],
+            recv_sem=q_recv.at[c, d - 1],
             device_id=(b, target),
             device_id_type=MESH,
         )
 
-    def piece(j):
-        return own if j == 0 else far[j - 1].at[1]
-
-    def z_copy(j):
-        return pltpu.make_async_remote_copy(
-            src_ref=piece(j),
-            dst_ref=far[j].at[1],
-            send_sem=z_send.at[j],
-            recv_sem=z_recv.at[j],
+    def piece(j, part):
+        return own.at[part] if j == 0 else far[j - 1].at[1, part]
+
+    def z_copy(j, part):
+        return pltpu.make_async_remote_copy(
+            src_ref=piece(j, part),
+            dst_ref=far[j].at[1, part],
+            send_sem=z_send.at[j, part],
+            recv_sem=z_recv.at[j, part],
             device_id=(b + 2, h),
             device_id_type=MESH,
         )
 
-    def x_copy(j, t):
-        return pltpu.make_async_remote_copy(
-            src_ref=piece(j),
-            dst_ref=far[t].at[0],
-            send_sem=x_send.at[j],
-            recv_sem=x_recv.at[t],
+    def x_copy(j, t, part):
+        return pltpu.make_async_remote_copy(
+            src_ref=piece(j, part),
+            dst_ref=far[t].at[0, part],
+            send_sem=x_send.at[j, part],
+            recv_sem=x_recv.at[t, part],
             device_id=(partner, h),
             device_id_type=MESH,
         )
@@ -119,37 +122,38 @@
     def pass_on(j):
         if j >= half:
             return
-        if j:
-            @pl.when(b - 2 * j >= 0)
+        for part in range(2):
+            if j:
+                @pl.when(b - 2 * j >= 0)
+                def _():
+                    z_copy(j - 1, part).wait_recv()
+
+            @pl.when(z_sends(j))
             def _():
-                z_copy(j - 1).wait_recv()
-
-        @pl.when(z_sends(j))
-        def _():
-            z_copy(j).start()
-
-        @pl.when(jnp.logical_and(odd == 0, b - 2 * j >= 0))
-        def _():
-            x_copy(j, j).start()
-
-        if j:
-            @pl.when(jnp.logical_and(odd == 1, b - 2 * j >= 0))
+                z_copy(j, part).start()
+
+            @pl.when(jnp.logical_and(odd == 0, b - 2 * j >= 0))
             def _():
-                x_copy(j, j - 1).start()
+                x_copy(j, j, part).start()
+
+            if j:
+                @pl.when(jnp.logical_and(odd == 1, b - 2 * j >= 0))
+                def _():
+                    x_copy(j, j - 1, part).start()
 
     for part in range(2):
         for d in range(1, nh):
             kv_copy(d, part).start()
-    for d in range(1, nh):
-        q_copy(d).start()
     for part in range(2):
         for d in range(1, nh):
             kv_copy(d, part).wait_recv()
+    for c in range(2):
+        for d in range(1, nh):
+            q_copy(d, c).start()
 
     pass_on(0)
     pass_on(1)
-    for d in range(1, nh):
-        q_copy(d).wait_recv()
+    own_q.wait()
 
     tile_blocks = min(4, nh)
     tiles = nh // tile_blocks
@@ -183,36 +187,76 @@
             jnp.concatenate(values_turned, axis=1), joined, preferred_element_type=jnp.float32
         )
 
-    def near_step(g, carry):
-        head = h * hh + g
-        for n in range(nh):
+    near_pair = min(2, hh // 2)
+
+    def near_step(i, carry):
+        results = []
+        for u in range(near_pair):
+            g = i * near_pair + u
+            head = h * hh + g
+            for n in range(nh):
+                query = qbuf[n, :, lanes(g, HEAD_DIM)]
+                listed = near_ref[head, n]
+                live = listed >= 0
+                pick = jnp.maximum(listed, 0)
+                both = scores_of(jnp.concatenate([own[0, n], own[0, pick]], axis=0), query)
+                s0 = both[:BLOCK] + causal_bias
+                s1 = both[BLOCK:]
+                top = jnp.maximum(column_max(s0), jnp.where(live, column_max(s1), NEG))
+                w0 = weigh(s0, top)
+                w1 = weigh(s1, jnp.where(live, top, -NEG))
+                total = column_sum(w0) + column_sum(w1)
+                results.append((g, n, top, total, mix([own[1, n], own[1, pick]], [w0, w1])))
+        for g, n, top, total, mixed in results:
             tile, at = n // tile_blocks, n % tile_blocks * BLOCK
-            query = qbuf[n, :, lanes(g, HEAD_DIM)]
-            listed = near_ref[head, n]
-            live = listed >= 0
-            pick = jnp.maximum(listed, 0)
-            s0 = scores_of(own[0, n], query) + causal_bias
-            s1 = scores_of(own[0, pick], query)
-            top = jnp.maximum(column_max(s0), jnp.where(live, column_max(s1), NEG))
-            w0 = weigh(s0, top)
-            w1 = weigh(s1, jnp.where(live, top, -NEG))
             tops[g, tile, :, at : at + BLOCK] = top
-            sums[g, tile, :, at : at + BLOCK] = column_sum(w0) + column_sum(w1)
-            accs[g, tile, :, at : at + BLOCK] = mix([own[1, n], own[1, pick]], [w0, w1])
+            sums[g, tile, :, at : at + BLOCK] = total
+            accs[g, tile, :, at : at + BLOCK] = mixed
         return carry
 
-    lax.fori_loop(0, hh, near_step, 0)
+    steps = hh // 2 // near_pair
+    for c in range(2):
+        for d in range(1, nh):
+            q_copy(d, c).wait_recv()
+        lax.fori_loop(c * steps, (c + 1) * steps, near_step, 0)
+        pass_on(2 + c)
+
+    def last_step(g, carry):
+        for tile in range(tiles):
+            done = (accs[g, tile] / sums[g, tile]).astype(jnp.bfloat16)
+            for n in range(tile_blocks):
+                obuf[g, tile * tile_blocks + n] = done[:, n * BLOCK : (n + 1) * BLOCK].T
+        out_ref[:, lanes(h * hh + g, HEAD_DIM)] = obuf[g, h]
+        for d in range(1, nh):
+            o_copy(g, d).start()
+        return carry
 
     for t in range(half):
-        pass_on(t + 2)
+        pass_on(t + 4)
 
         @pl.when(b - 1 - 2 * t >= 0)
         def _(t=t):
-            x_copy(t, t).wait_recv()
+            x_copy(t, t, 0).wait_recv()
+            x_copy(t, t, 1).wait_recv()
             slots = (0, (b - 2 - 2 * t >= 0).astype(jnp.int32))
 
             def far_step(i, carry):
-                g, tile = lax.div(i, tiles), lax.rem(i, tiles)
+                first, tile = lax.div(i, tiles) * far_pair, lax.rem(i, tiles)
+                heads_now = [first + u for u in range(far_pair)]
+                results = [far_tile(g, tile) for g in heads_now]
+                for g, (top, total, acc) in zip(heads_now, results):
+                    tops[g, tile] = top
+                    sums[g, tile] = total
+                    accs[g, tile] = acc
+
+                @pl.when(jnp.logical_and(b - 3 - 2 * t < 0, tile == tiles - 1))
+                def _():
+                    for g in heads_now:
+                        last_step(g, 0)
+
+                return carry
+
+            def far_tile(g, tile):
                 head = h * hh + g
                 query_rows = jnp.concatenate(
                     [
@@ -221,45 +265,38 @@
                     ],
                     axis=0,
                 )
-                lives, values_turned, scores = [], [], []
-                top = tops[g, tile]
-                new_top = top
+                lives, keys_here, values_turned = [], [], []
                 for e in range(4):
                     r = b - 1 - 2 * t - e // 2
                     listed = vert_ref[head, jnp.maximum(r, 0), e % 2]
                     pick = jnp.maximum(listed, 0)
                     slot = slots[e // 2]
-                    live = jnp.logical_and(listed >= 0, r >= 0)
-                    lives.append(live)
+                    lives.append(jnp.logical_and(listed >= 0, r >= 0))
+                    keys_here.append(far[t][slot, 0, pick])
                     values_turned.append(far[t][slot, 1, pick])
-                    s = scores_of(far[t][slot, 0, pick], query_rows)
-                    scores.append(s)
-                    new_top = jnp.maximum(new_top, jnp.where(live, column_max(s), NEG))
+                every = scores_of(jnp.concatenate(keys_here, axis=0), query_rows)
+                top = tops[g, tile]
+                new_top = top
+                for e in range(4):
+                    peak = column_max(every[e * BLOCK : (e + 1) * BLOCK])
+                    new_top = jnp.maximum(new_top, jnp.where(lives[e], peak, NEG))
                 shrink = weigh(top, new_top)
                 total = sums[g, tile] * shrink
                 weights = []
-                for live, s in zip(lives, scores):
-                    w = weigh(s, jnp.where(live, new_top, -NEG))
+                for e in range(4):
+                    w = weigh(
+                        every[e * BLOCK : (e + 1) * BLOCK], jnp.where(lives[e], new_top, -NEG)
+                    )
                     total = total + column_sum(w)
                     weights.append(w)
-                tops[g, tile] = new_top
-                sums[g, tile] = total
-                accs[g, tile] = accs[g, tile] * shrink + mix(values_turned, weights)
-                return carry
-
-            lax.fori_loop(0, hh * tiles, far_step, 0)
-
-    def last_step(g, carry):
-        for tile in range(tiles):
-            done = (accs[g, tile] / sums[g, tile]).astype(jnp.bfloat16)
-            for n in range(tile_blocks):
-                obuf[g, tile * tile_blocks + n] = done[:, n * BLOCK : (n + 1) * BLOCK].T
-        out_ref[:, lanes(h * hh + g, HEAD_DIM)] = obuf[g, h]
-        for d in range(1, nh):
-            o_copy(g, d).start()
-        return carry
-
-    lax.fori_loop(0, hh, last_step, 0)
+                return new_top, total, accs[g, tile] * shrink + mix(values_turned, weights)
+
+            far_pair = min(2, hh)
+            lax.fori_loop(0, hh // far_pair * tiles, far_step, 0)
+
+    @pl.when(b == 0)
+    def _():
+        lax.fori_loop(0, hh, last_step, 0)
 
     def finish(g, carry):
         for d in range(1, nh):
@@ -278,15 +315,17 @@
     for d in range(1, nh):
         kv_copy(d, 0).wait_send()
         kv_copy(d, 1).wait_send()
-        q_copy(d).wait_send()
+        q_copy(d, 0).wait_send()
+        q_copy(d, 1).wait_send()
     for j in range(half):
-        @pl.when(z_sends(j))
-        def _():
-            z_copy(j).wait_send()
-
-        @pl.when(b - 2 * j >= (0 if j else 2 * odd * nb))
-        def _():
-            x_copy(j, 0).wait_send()
+        for part in range(2):
+            @pl.when(z_sends(j))
+            def _():
+                z_copy(j, part).wait_send()
+
+            @pl.when(b - 2 * j >= (0 if j else 2 * odd * nb))
+            def _():
+                x_copy(j, 0, part).wait_send()
 
 
 def local(queries, keys, values, vertical, near):
@@ -302,7 +341,7 @@
     return pl.pallas_call(
         functools.partial(kernel, nb, nh),
         out_shape=jax.ShapeDtypeStruct((BLOCK, QHEADS * HEAD_DIM), jnp.bfloat16),
-        in_specs=[vmem, vmem, vmem, smem, smem],
+        in_specs=[pl.BlockSpec(memory_space=pl.ANY), vmem, vmem, smem, smem],
         out_specs=vmem,
         scratch_shapes=[pltpu.VMEM((2, 2, nh, BLOCK, HEAD_DIM), jnp.bfloat16)] * half
         + [
@@ -315,14 +354,15 @@
             pltpu.VMEM((hh, tiles, HEAD_DIM, nh // tiles * BLOCK), jnp.float32),
             dma((2, nh - 1)),
             dma((2, nh - 1)),
-            dma((nh - 1,)),
-            dma((nh - 1,)),
-            dma((half,)),
-            dma((half,)),
-            dma((half,)),
-            dma((half,)),
+            dma((2, nh - 1)),
+            dma((2, nh - 1)),
+            dma((half, 2)),
+            dma((half, 2)),
+            dma((half, 2)),
+            dma((half, 2)),
             dma((hh, nh - 1)),
             dma((hh, nh - 1)),
+            dma,
         ],
         compiler_params=pltpu.CompilerParams(
             collective_id=0, has_side_effects=True, vmem_limit_bytes=48 * 1024 * 1024

time: 64.9 us -> 60.8 us (0.937)
  Pallas kernels: 60.7 us -> 56.1 us
    pallas_call x1, Pallas kernels: 60.7 us -> 56.1 us  [local(): pl.pallas_call(functools.partial(kernel, nb, nh), out_shape=jax.ShapeDtyp...]
where the time goes in v3:
time: 60.8 us; the launch traced here: 60.1 us
  Pallas kernels  56.1 us (92%)
  local copies, waits for them, and re-layouts  4.04 us (7%)
    pallas_call x1, Pallas kernels, local(): pl.pallas_call(functools.partial(kernel, nb, nh), out_shape=jax.ShapeDtyp...  56.1 us
    unnamed x11, local copies, waits for them, and re-layouts  4.04 us

profile of v3, /device:TPU:31, one launch (start us, length us, event | category | flops | bytes accessed | tf_op | source)
XLA Modules:
  0.0 60.1 jit_solution(16240874592351156750)
XLA Ops:
  0.0 0.0 copy-start.3
  0.0 0.0 copy-start.1
  0.0 0.8 %copy.7.near_ref = s32[32,4]{1,0:T(8,128)S(1)} copy(s32[32,4]{0,1:T(4,128)} %param.9) | data formatting | bytes 1024 | tf_op args[4]
  0.8 0.0 copy-done.3
  0.8 0.1 copy.6.vert_ref
  0.9 0.0 copy-done.1
  1.0 0.0 copy-start
  1.0 1.2 %copy-done = bf16[128,4096]{1,0:T(8,128)(2,1)S(1)} copy-done((bf16[128,4096]{1,0:T(8,128)(2,1)S(1)}, bf16[128,4096]{1,0:T(8,128)(2,1)}, u32[]{:S(2)}) %copy-start) | copy-done | bytes 1048600
  2.2 0.0 copy-start.2
  2.2 0.9 %copy-done.2 = bf16[128,512]{1,0:T(8,128)(2,1)S(1)} copy-done((bf16[128,512]{1,0:T(8,128)(2,1)S(1)}, bf16[128,512]{1,0:T(8,128)(2,1)}, u32[]{:S(2)}) %copy-start.2) | copy-done | bytes 131096
  3.1 56.1 %shard_map.55 = bf16[128,4096]{1,0:T(8,128)(2,1)S(1)} custom-call(bf16[128,4096]{1,0:T(8,128)(2,1)S(1)} %copy-done, bf16[128,512]{1,0:T(8,128)(2,1)S(1)} %copy-done.1, bf16[128,512]{1,0:T(8,128)(2,1)S(1)} %copy-done.2, s32[32,8,2]{2,1,0:T(8,128)S(1)} %copy.6.vert_ref, s32[32,4]{1,0:T(8,128)S(1)} %copy.7.near_ref), custom_call_target="tpu_custom_call" | custom-call | tf_op jit(solution)/shard_map/pallas_call | solution.py:341
  59.1 1.0 %copy.9 = bf16[128,4096]{1,0:T(8,128)(2,1)} copy(bf16[128,4096]{1,0:T(8,128)(2,1)S(1)} %shard_map.55) | data formatting | bytes 2097152
Async XLA Ops:
  0.0 0.8 %copy-start.3 = (s32[32,8,2]{0,2,1:T(2,128)S(1)}, s32[32,8,2]{0,2,1:T(2,128)}, u32[]{:S(2)}) copy-start(s32[32,8,2]{0,2,1:T(2,128)} %param.8) | copy-start | bytes 6148
  0.0 0.9 %copy-start.1 = (bf16[128,512]{1,0:T(8,128)(2,1)S(1)}, bf16[128,512]{1,0:T(8,128)(2,1)}, u32[]{:S(2)}) copy-start(bf16[128,512]{1,0:T(8,128)(2,1)} %k_ref.1) | copy-start | bytes 393220
  1.0 1.2 %copy-start = (bf16[128,4096]{1,0:T(8,128)(2,1)S(1)}, bf16[128,4096]{1,0:T(8,128)(2,1)}, u32[]{:S(2)}) copy-start(bf16[128,4096]{1,0:T(8,128)(2,1)} %q_ref.1) | copy-start | bytes 3145732
  2.2 0.9 %copy-start.2 = (bf16[128,512]{1,0:T(8,128)(2,1)S(1)}, bf16[128,512]{1,0:T(8,128)(2,1)}, u32[]{:S(2)}) copy-start(bf16[128,512]{1,0:T(8,128)(2,1)} %v_ref.1) | copy-start | bytes 393220

commit v4 on v3

--- a/solution.py
+++ b/solution.py
@@ -15,13 +15,10 @@
 NEG = -1e30
 EXP2_SCALE = math.log2(math.e) / math.sqrt(HEAD_DIM)
 MESH = pl.DeviceIdType.MESH
-CONTRACT_LAST = (((1,), (1,)), ((), ()))
-
-
-def scores_of(query_rows, key_rows):
-    return lax.dot_general(
-        query_rows, key_rows, CONTRACT_LAST, preferred_element_type=jnp.float32
-    )
+
+
+def scores_of(key_rows, query_turned):
+    return jnp.dot(key_rows, query_turned, preferred_element_type=jnp.float32)
 
 
 def kernel(nb, nh, q_ref, k_ref, v_ref, vert_ref, near_ref, out_ref, *scratch):
@@ -29,12 +26,11 @@
     far, scratch = scratch[:half], scratch[half:]
     qbuf, own, vturn, obuf, tops, sums, accs = scratch[:7]
     kv_send, kv_recv, q_send, q_recv, z_send, z_recv, x_send, x_recv, o_send, o_recv = scratch[7:17]
-    local_sem = scratch[17]
+    local_sem, qrows, qturn = scratch[17:]
     b = lax.axis_index("blk")
     h = lax.axis_index("head")
     hh = QHEADS // nh
     rep = nh // KVHEADS
-    width = hh * HEAD_DIM
     odd = lax.rem(b, 2)
     partner = b + 1 - 2 * odd
 
@@ -62,8 +58,8 @@
     for kv in range(KVHEADS):
         vturn[kv] = v_ref[:, kv * HEAD_DIM : (kv + 1) * HEAD_DIM].T
     own[1, h] = vturn[mine]
-    own_q = pltpu.make_async_copy(q_ref.at[:, lanes(h, width)], qbuf.at[h], local_sem)
-    own_q.start()
+    fetch = pltpu.make_async_copy(q_ref, qrows, local_sem)
+    fetch.start()
 
     pl.semaphore_wait(
         barrier, nh + (b + 2 < nb).astype(jnp.int32) + (b >= 2).astype(jnp.int32)
@@ -83,10 +79,10 @@
 
     def q_copy(d, c):
         target = peer(d)
-        part = width // 2
-        return pltpu.make_async_remote_copy(
-            src_ref=q_ref.at[:, pl.ds(pl.multiple_of(target * width + c * part, part), part)],
-            dst_ref=qbuf.at[h, :, pl.ds(c * part, part)],
+        count = hh // 2
+        return pltpu.make_async_remote_copy(
+            src_ref=qturn.at[pl.ds(target * hh + c * count, count)],
+            dst_ref=qbuf.at[h, pl.ds(c * count, count)],
             send_sem=q_send.at[c, d - 1],
             recv_sem=q_recv.at[c, d - 1],
             device_id=(b, target),
@@ -144,6 +140,16 @@
     for part in range(2):
         for d in range(1, nh):
             kv_copy(d, part).start()
+    fetch.wait()
+
+    def turn_step(i, carry):
+        for u in range(4):
+            qturn[i * 4 + u] = qrows[:, pl.ds(pl.multiple_of((i * 4 + u) * BLOCK, BLOCK), BLOCK)].T
+        return carry
+
+    lax.fori_loop(0, QHEADS // 4, turn_step, 0)
+    for g in range(hh):
+        qbuf[h, g] = qturn[h * hh + g]
     for part in range(2):
         for d in range(1, nh):
             kv_copy(d, part).wait_recv()
@@ -153,7 +159,6 @@
 
     pass_on(0)
     pass_on(1)
-    own_q.wait()
 
     tile_blocks = min(4, nh)
     tiles = nh // tile_blocks
@@ -195,7 +200,7 @@
             g = i * near_pair + u
             head = h * hh + g
             for n in range(nh):
-                query = qbuf[n, :, lanes(g, HEAD_DIM)]
+                query = qbuf[n, g]
                 listed = near_ref[head, n]
                 live = listed >= 0
                 pick = jnp.maximum(listed, 0)
@@ -258,12 +263,12 @@
 
             def far_tile(g, tile):
                 head = h * hh + g
-                query_rows = jnp.concatenate(
+                query_turned = jnp.concatenate(
                     [
-                        qbuf[tile * tile_blocks + n, :, lanes(g, HEAD_DIM)]
+                        qbuf[tile * tile_blocks + n, g]
                         for n in range(tile_blocks)
                     ],
-                    axis=0,
+                    axis=1,
                 )
                 lives, keys_here, values_turned = [], [], []
                 for e in range(4):
@@ -274,7 +279,7 @@
                     lives.append(jnp.logical_and(listed >= 0, r >= 0))
                     keys_here.append(far[t][slot, 0, pick])
                     values_turned.append(far[t][slot, 1, pick])
-                every = scores_of(jnp.concatenate(keys_here, axis=0), query_rows)
+                every = scores_of(jnp.concatenate(keys_here, axis=0), query_turned)
                 top = tops[g, tile]
                 new_top = top
                 for e in range(4):
@@ -345,7 +350,7 @@
         out_specs=vmem,
         scratch_shapes=[pltpu.VMEM((2, 2, nh, BLOCK, HEAD_DIM), jnp.bfloat16)] * half
         + [
-            pltpu.VMEM((nh, BLOCK, hh * HEAD_DIM), jnp.bfloat16),
+            pltpu.VMEM((nh, hh, HEAD_DIM, BLOCK), jnp.bfloat16),
             pltpu.VMEM((2, nh, BLOCK, HEAD_DIM), jnp.bfloat16),
             pltpu.VMEM((KVHEADS, HEAD_DIM, BLOCK), jnp.bfloat16),
             pltpu.VMEM((hh, nh, BLOCK, HEAD_DIM), jnp.bfloat16),
@@ -363,6 +368,8 @@
             dma((hh, nh - 1)),
             dma((hh, nh - 1)),
             dma,
+            pltpu.VMEM((BLOCK, QHEADS * HEAD_DIM), jnp.bfloat16),
+            pltpu.VMEM((QHEADS, HEAD_DIM, BLOCK), jnp.bfloat16),
         ],
         compiler_params=pltpu.CompilerParams(
             collective_id=0, has_side_effects=True, vmem_limit_bytes=48 * 1024 * 1024

time: 60.8 us -> 60.4 us (level)
  no operation moved by 1% of the time
where the time goes in v4:
time: 60.4 us; the launch traced here: 59.7 us
  Pallas kernels  55.7 us (92%)
  local copies, waits for them, and re-layouts  4.04 us (7%)
    pallas_call x1, Pallas kernels, local(): pl.pallas_call(functools.partial(kernel, nb, nh), out_shape=jax.ShapeDtyp...  55.7 us
    unnamed x11, local copies, waits for them, and re-layouts  4.04 us

profile of v4, /device:TPU:31, one launch (start us, length us, event | category | flops | bytes accessed | tf_op | source)
XLA Modules:
  0.0 59.7 jit_solution(16964207713699116934)
XLA Ops:
  0.0 0.0 copy-start.3
  0.0 0.0 copy-start.1
  0.0 0.8 %copy.7.near_ref = s32[32,4]{1,0:T(8,128)S(1)} copy(s32[32,4]{0,1:T(4,128)} %param.9) | data formatting | bytes 1024 | tf_op args[4]
  0.8 0.0 copy-done.3
  0.8 0.1 copy.6.vert_ref
  0.9 0.0 copy-done.1
  1.0 0.0 copy-start
  1.0 1.2 %copy-done = bf16[128,4096]{1,0:T(8,128)(2,1)S(1)} copy-done((bf16[128,4096]{1,0:T(8,128)(2,1)S(1)}, bf16[128,4096]{1,0:T(8,128)(2,1)}, u32[]{:S(2)}) %copy-start) | copy-done | bytes 1048600
  2.2 0.0 copy-start.2
  2.2 0.9 %copy-done.2 = bf16[128,512]{1,0:T(8,128)(2,1)S(1)} copy-done((bf16[128,512]{1,0:T(8,128)(2,1)S(1)}, bf16[128,512]{1,0:T(8,128)(2,1)}, u32[]{:S(2)}) %copy-start.2) | copy-done | bytes 131096
  3.1 55.7 %shard_map.55 = bf16[128,4096]{1,0:T(8,128)(2,1)S(1)} custom-call(bf16[128,4096]{1,0:T(8,128)(2,1)S(1)} %copy-done, bf16[128,512]{1,0:T(8,128)(2,1)S(1)} %copy-done.1, bf16[128,512]{1,0:T(8,128)(2,1)S(1)} %copy-done.2, s32[32,8,2]{2,1,0:T(8,128)S(1)} %copy.6.vert_ref, s32[32,4]{1,0:T(8,128)S(1)} %copy.7.near_ref), custom_call_target="tpu_custom_call" | custom-call | tf_op jit(solution)/shard_map/pallas_call | solution.py:346
  58.8 1.0 %copy.9 = bf16[128,4096]{1,0:T(8,128)(2,1)} copy(bf16[128,4096]{1,0:T(8,128)(2,1)S(1)} %shard_map.55) | data formatting | bytes 2097152
Async XLA Ops:
  0.0 0.8 %copy-start.3 = (s32[32,8,2]{0,2,1:T(2,128)S(1)}, s32[32,8,2]{0,2,1:T(2,128)}, u32[]{:S(2)}) copy-start(s32[32,8,2]{0,2,1:T(2,128)} %param.8) | copy-start | bytes 6148
  0.0 0.9 %copy-start.1 = (bf16[128,512]{1,0:T(8,128)(2,1)S(1)}, bf16[128,512]{1,0:T(8,128)(2,1)}, u32[]{:S(2)}) copy-start(bf16[128,512]{1,0:T(8,128)(2,1)} %k_ref.1) | copy-start | bytes 393220
  1.0 1.2 %copy-start = (bf16[128,4096]{1,0:T(8,128)(2,1)S(1)}, bf16[128,4096]{1,0:T(8,128)(2,1)}, u32[]{:S(2)}) copy-start(bf16[128,4096]{1,0:T(8,128)(2,1)} %q_ref.1) | copy-start | bytes 3145732
  2.2 0.9 %copy-start.2 = (bf16[128,512]{1,0:T(8,128)(2,1)S(1)}, bf16[128,512]{1,0:T(8,128)(2,1)}, u32[]{:S(2)}) copy-start(bf16[128,512]{1,0:T(8,128)(2,1)} %v_ref.1) | copy-start | bytes 393220
